TPU v7x, 32 devices: a whole 2x2x4 slice. The times are simulated.
32 devices in a mesh: dp: 4 (over y, x), expert: 8 (over z, core).
Axes of the slice: x: 2, y: 2, z: 4, core: 2. Of those that a mesh axis runs over, the one named last changes fastest.
Arguments:
- tokens: bfloat16 [4, 1024, 1280], P('dp', 'expert'), may hold values from -6 to 6
- cotangent: bfloat16 [4, 1024, 1280], P('dp', 'expert'), may hold values from -6 to 6
- attn_gain: bfloat16 [1280], P('expert'), may hold values from 0.099609375 to 1.8984375
- ffn_gain: bfloat16 [1280], P('expert'), may hold values from 0.099609375 to 1.8984375
- w_query: bfloat16 [1280, 1280], P('expert'), may hold values from -0.15625 to 0.15625
- w_key: bfloat16 [1280, 1280], P('expert'), may hold values from -0.15625 to 0.15625
- w_value: bfloat16 [1280, 1280], P('expert'), may hold values from -0.15625 to 0.15625
- w_output: bfloat16 [1280, 1280], P('expert'), may hold values from -2.5 to 2.5
- router: bfloat16 [1280, 16], P('expert'), may hold values from -0.078125 to 0.078125
- shared_gate: bfloat16 [1280, 896], P('expert'), may hold values from -0.15625 to 0.15625
- shared_up: bfloat16 [1280, 896], P('expert'), may hold values from -0.15625 to 0.15625
- shared_down: bfloat16 [896, 1280], P('expert'), may hold values from -0.1875 to 0.1875
- expert_gate: bfloat16 [16, 1280, 896], P('expert'), may hold values from -0.15625 to 0.15625
- expert_up: bfloat16 [16, 1280, 896], P('expert'), may hold values from -0.15625 to 0.15625
- expert_down: bfloat16 [16, 896, 1280], P('expert'), may hold values from -12 to 12
- expert_ids: int32 [32, 128, 6], P(('dp', 'expert')), may hold values from 0 to 15, all different within a row; in each aligned block of 128 rows (0 to 127, 128 to 255, ..., all dimensions but the last counted through in order) at most 96 rows name the same one
Outputs:
- layer_output: bfloat16 [4, 1024, 1280], P('dp', 'expert')
- input_grad: bfloat16 [4, 1024, 1280], P('dp', 'expert')
- attn_gain_grad: float32 [1280], P('expert')
- ffn_gain_grad: float32 [1280], P('expert')
- query_grad: float32 [1280, 1280], P('expert')
- key_grad: float32 [1280, 1280], P('expert')
- value_grad: float32 [1280, 1280], P('expert')
- output_grad: float32 [1280, 1280], P('expert')
- router_grad: float32 [1280, 16], P('expert')
- shared_gate_grad: float32 [1280, 896], P('expert')
- shared_up_grad: float32 [1280, 896], P('expert')
- shared_down_grad: float32 [896, 1280], P('expert')
- expert_gate_grad: float32 [16, 1280, 896], P('expert')
- expert_up_grad: float32 [16, 1280, 896], P('expert')
- expert_down_grad: float32 [16, 896, 1280], P('expert')
Inputs may be any that keep to these rules, and one draw needn't show every extreme that they name: `expert_ids`: in each block of 128 rows (one value of the first dimension) no expert is named more than 96 times, a bound that some block reaches; the 6 ids of a token differ.
All inputs are finite; a program needn't handle non-finite values.
Results may differ from a plain program's by a relative error of at most 0.02.
Values may be sent and summed in bfloat16 or wider, within the bound.
A program may use at most 320 MiB of HBM per device.

v0:
```python
import functools

import jax
import jax.numpy as jnp
import numpy as np
from jax import lax
from jax.experimental import pallas as pl
from jax.experimental.pallas import tpu as pltpu
from jax.sharding import PartitionSpec as P

HEAD_DIM = 128
LANES = 128
TURNED = 16
EPS = 1e-06
MASKED = -1e30
VMEM_LIMIT = 60 * 2**20
BF = jnp.bfloat16
F32 = jnp.float32


def dot(a, b):
    return jnp.dot(a, b, preferred_element_type=F32)


def dot_nt(a, b):
    return lax.dot_general(a, b, (((1,), (1,)), ((), ())), preferred_element_type=F32)


def dot_tn(a, b):
    return lax.dot_general(a, b, (((0,), (0,)), ((), ())), preferred_element_type=F32)


def silu(v):
    return v / (1.0 + jnp.exp(-v))


def swiglu_back(d_hidden, gates, ups):
    sigma = 1.0 / (1.0 + jnp.exp(-gates))
    d_gate = d_hidden * ups * sigma * (1.0 + gates * (1.0 - sigma))
    d_up = d_hidden * (gates * sigma)
    return d_gate.astype(BF), d_up.astype(BF)


def rotary_tables(length):
    half = HEAD_DIM // 2
    inverse_freq = np.float32(10000.0) ** (-np.arange(half, dtype=np.float32) * np.float32(2.0 / HEAD_DIM))
    angles = np.arange(length, dtype=np.float32)[:, None] * inverse_freq[None, :]
    cosine, sine = np.cos(angles), np.sin(angles)
    tables = np.concatenate([cosine, cosine], -1), np.concatenate([-sine, sine], -1)
    return tuple(jnp.asarray(t.astype(np.float32)) for t in tables)


def vmem_call(kernel, outs, *args, **kwargs):
    spec = pl.BlockSpec(memory_space=pltpu.VMEM)
    return pl.pallas_call(
        kernel,
        out_shape=outs,
        in_specs=[spec] * len(args),
        out_specs=[spec] * len(outs),
        compiler_params=pltpu.CompilerParams(vmem_limit_bytes=VMEM_LIMIT),
        **kwargs,
    )(*args)


def row_block(length):
    return 256 if length % 256 == 0 else length


def remote(src, dst, send, recv, **device):
    return pltpu.make_async_remote_copy(
        src_ref=src, dst_ref=dst, send_sem=send, recv_sem=recv, device_id=device, device_id_type=pl.DeviceIdType.MESH
    )


def meet(peers):
    barrier = pltpu.get_barrier_semaphore()
    for peer in peers:
        pl.semaphore_signal(barrier, inc=1, device_id=peer, device_id_type=pl.DeviceIdType.MESH)
    pl.semaphore_wait(barrier, len(peers))


def meet_near(chips, z, me, peers=()):
    barrier = pltpu.get_barrier_semaphore()
    near = [(True, {"expert": me + 1 - 2 * lax.rem(me, 2)}), (z > 0, {"expert": me - 2}), (z < chips - 1, {"expert": me + 2})]
    near += [(True, {"dp": t}) for t in peers]

    def signal(t):
        pl.semaphore_signal(barrier, inc=1, device_id=t, device_id_type=pl.DeviceIdType.MESH)

    for ok, t in near:
        guarded(ok, functools.partial(signal, t))
    ends = jnp.where(z > 0, 1, 0) + jnp.where(z < chips - 1, 1, 0)
    pl.semaphore_wait(barrier, 1 + len(peers) + ends)


def both(*conditions):
    held = [c for c in conditions if c is not True]
    if not held:
        return True
    out = held[0]
    for c in held[1:]:
        out = jnp.logical_and(out, c)
    return out


def guarded(condition, action):
    if condition is True:
        action()
    else:
        pl.when(condition)(action)


class LineGather:
    def __init__(self, ranks, own, block, send, recv, base=0, valid=lambda i: True, twins=True):
        self.me = lax.axis_index("expert")
        self.chips = ranks // 2
        self.z = self.me // 2
        self.twin = self.me + 1 - 2 * lax.rem(self.me, 2)
        self.own, self.block, self.send, self.recv, self.base, self.valid = own, block, send, recv, base, valid
        self.twins = twins

    @staticmethod
    def semaphores(ranks):
        return 4 * (ranks // 2 - 1) + 1

    def copy(self, src, i, k, to):
        return remote(src, self.block(i), self.send.at[self.base + k], self.recv.at[self.base + k], expert=to)

    def sources(self, s):
        hops = self.chips - 1
        return (
            (self.me - 2 * s, self.z - s >= 0, self.z < hops, self.me + 2, 0, 2 * hops, -2 * s),
            (self.me + 2 * s, self.z + s <= hops, self.z > 0, self.me - 2, hops, 3 * hops, 2 * s),
        )

    def start(self):
        hops = self.chips - 1
        mine = self.valid(self.me)
        if hops:
            guarded(both(self.z < hops, mine), lambda: self.copy(self.own, self.me, 0, self.me + 2).start())
            guarded(both(self.z > 0, mine), lambda: self.copy(self.own, self.me, hops, self.me - 2).start())
        if self.twins:
            guarded(mine, lambda: self.copy(self.own, self.me, 2 * hops, self.twin).start())

    def step(self, s):
        for i, there, more, to, k, pair, _ in self.sources(s):
            known = both(there, self.valid(i))
            src = self.block(i)
            guarded(known, lambda: self.copy(src, i, k + s - 1, self.twin).wait_recv())
            if s < self.chips - 1:
                guarded(both(known, more), lambda: self.copy(src, i, k + s, to).start())
            if self.twins:
                guarded(known, lambda: self.copy(src, i, pair + s, self.twin).start())

    def finish(self):
        hops = self.chips - 1
        mine = self.valid(self.me)
        theirs = self.valid(self.twin)
        if self.twins:
            guarded(mine, lambda: self.copy(self.own, self.me, 2 * hops, self.twin).wait_send())
            guarded(theirs, lambda: self.copy(self.own, self.twin, 2 * hops, self.twin).wait_recv())
        if hops:
            guarded(both(self.z < hops, mine), lambda: self.copy(self.own, self.me, 0, self.twin).wait_send())
            guarded(both(self.z > 0, mine), lambda: self.copy(self.own, self.me, hops, self.twin).wait_send())
        for s in range(1, self.chips):
            for i, there, more, to, k, pair, shift in self.sources(s):
                known = both(there, self.valid(i))
                src = self.block(i)
                if s < hops:
                    guarded(both(known, more), lambda: self.copy(src, i, k + s, self.twin).wait_send())
                if not self.twins:
                    continue
                guarded(known, lambda: self.copy(src, i, pair + s, self.twin).wait_send())
                j = self.twin + shift
                got = both(there, self.valid(j))
                guarded(got, lambda: self.copy(self.block(j), j, pair + s, self.twin).wait_recv())


class Across:
    SEMAPHORES = 12

    def __init__(self, source, dst, send, recv):
        self.me, self.g = lax.axis_index("expert"), lax.axis_index("dp")
        self.twin = self.me + 1 - 2 * lax.rem(self.me, 2)
        self.by_x = self.g + 1 - 2 * lax.rem(self.g, 2)
        self.by_y = lax.rem(self.g + 2, 4)
        self.source, self.dst, self.send, self.recv = source, dst, send, recv
        self.half = dst.shape[1]
        self.part = self.half // 2

    def peers(self):
        return [{"dp": self.by_x}, {"dp": self.by_y}, {"expert": self.twin}]

    def piece(self, slot, j):
        return self.dst.at[slot, pl.ds(j * self.part, self.part)]

    def mine(self, j):
        first = lax.rem(self.me, 2) * self.half + j * self.part
        return self.source(pl.ds(pl.multiple_of(first, self.part), self.part))

    def copy(self, k, src, dst, **to):
        return remote(src, dst, self.send.at[k], self.recv.at[k], **to)

    def direct(self, k):
        slot, j, to = ((0, 0, self.by_x), (1, 1, self.by_y), (0, 1, self.by_x), (1, 0, self.by_y))[k]
        return self.copy(k, self.mine(j), self.piece(slot, j), dp=to)

    def relayed(self, j):
        if j == 0:
            return self.copy(4, self.piece(0, 0), self.piece(2, 0), dp=self.by_y)
        return self.copy(5, self.piece(1, 1), self.piece(2, 1), dp=self.by_x)

    def shared(self, slot, j):
        return self.copy(6 + 2 * slot + j, self.piece(slot, j), self.piece(slot + 3, j), expert=self.twin)

    def start(self):
        for k in range(2):
            self.direct(k).start()

    def more(self):
        for k in range(2, 4):
            self.direct(k).start()

    def relay(self):
        self.direct(0).wait_recv()
        self.relayed(0).start()
        self.direct(1).wait_recv()
        self.relayed(1).start()
        self.shared(0, 0).start()
        self.shared(1, 1).start()

    def hand_over(self):
        self.direct(2).wait_recv()
        self.shared(0, 1).start()
        self.direct(3).wait_recv()
        self.shared(1, 0).start()

    def finish(self):
        for j in range(2):
            self.relayed(j).wait_recv()
            self.shared(2, j).start()
        for k in range(4):
            self.direct(k).wait_send()
        for j in range(2):
            self.relayed(j).wait_send()
            for slot in range(3):
                self.shared(slot, j).wait()


class SameExperts:
    SEMAPHORES = 6

    def __init__(self, source, dst, send, recv):
        self.me, self.g = lax.axis_index("expert"), lax.axis_index("dp")
        self.near = [self.g + 1 - 2 * lax.rem(self.g, 2), lax.rem(self.g + 2, 4)]
        self.near.append(self.near[1] + 1 - 2 * lax.rem(self.near[1], 2))
        self.source, self.dst, self.send, self.recv = source, dst, send, recv
        self.half = dst.shape[2]

    def peers(self):
        return [{"dp": self.near[2]}]

    def copy(self, k, h):
        slot = k + 3 * lax.rem(lax.rem(self.me, 2) + h, 2)
        i = 2 * k + h
        src = self.source.at[:, pl.ds(h * self.half, self.half)]
        return remote(src, self.dst.at[slot], self.send.at[i], self.recv.at[i], dp=self.near[k])

    def start(self):
        for k in range(3):
            for h in range(2):
                self.copy(k, h).start()

    def relay(self):
        pass

    hand_over = more = relay

    def finish(self):
        for k in range(3):
            for h in range(2):
                self.copy(k, h).wait()


def head_of(s, i, ranks):
    return i if s == 0 else s * ranks + i // 2 + (i % 2) * (ranks // 2)


def aligned(i, size):
    return pl.ds(pl.multiple_of(i * size, size), size)


def front_kernel(
    ranks, groups, heads, seqs, slots, gain_at,
    x_ref, c_ref, id_ref, wq_ref, wk_ref, wv_ref, sg_ref, su_ref, rest_ref, wo_ref, cos_ref, sin_ref,
    gx_ref, gc_ref, wqs_ref, wks_ref, wvs_ref, wps_ref, small_ref, half_ref,
    inv_ref, q_ref, k_ref, v_ref, mixed_ref, lse_ref, stage_ref, land_ref, ostage_ref,
    x_send, x_recv, c_send, c_recv, w_send, w_recv, d_send, d_recv, o_send, o_recv, p_send, p_recv,
):
    me, g = lax.axis_index("expert"), lax.axis_index("dp")
    rows, width = wq_ref.shape
    units = width // LANES
    per = ostage_ref.shape[0]
    peers = [lax.rem(g + d, groups) for d in range(1, groups)]
    others = [lax.rem(me + d, ranks) for d in range(1, ranks)]
    meet([{"expert": t} for t in others] + [{"dp": t} for t in peers])

    def stage_heads(w):
        for u in range(heads):
            stage_ref[u] = w[:, u * LANES : (u + 1) * LANES]

    for which, w in enumerate((wq_ref, wk_ref, wv_ref)):
        pl.when(g == which)(functools.partial(stage_heads, w))

    def stage_pack():
        share = sg_ref.shape[1] // ranks
        spare = slots * LANES - 2 * share - rest_ref.shape[1]
        for t in range(ranks):
            cols = slice(t * share, (t + 1) * share)
            pieces = [sg_ref[:, cols], su_ref[:, cols], rest_ref[...]]
            if spare:
                pieces.append(jnp.zeros((rows, spare), BF))
            packed = jnp.concatenate(pieces, -1)
            for s in range(slots):
                stage_ref[head_of(s, t, ranks)] = packed[:, s * LANES : (s + 1) * LANES]

    pl.when(g == groups - 1)(stage_pack)

    def known(s, t, group=None):
        return jnp.logical_or((g if group is None else group) == groups - 1, head_of(s, t, ranks) < heads)

    def weight_copy(s, d, unit, i, to):
        return remote(
            stage_ref.at[unit], land_ref.at[g, s, i], w_send.at[s, d], w_recv.at[s, d], expert=to
        )

    for d in range(1, ranks):
        t = others[d - 1]
        for s in range(slots):
            guarded(known(s, t), lambda: weight_copy(s, d, head_of(s, t, ranks), me, t).start())

    def stage_out(which):
        for k in range(per):
            u = which * per + k
            if u < units:
                ostage_ref[k] = wo_ref[:, u * LANES : (u + 1) * LANES]

    for which in range(groups):
        pl.when(g == which)(functools.partial(stage_out, which))
    out_rows = LineGather(
        ranks, ostage_ref, lambda i: half_ref.at[g, :, i // 2], o_send, o_recv, twins=False
    )
    out_rows.start()
    tokens = LineGather(ranks, x_ref, lambda i: gx_ref.at[i], x_send, x_recv)
    tokens.start()
    half_ref[g, :, me // 2] = ostage_ref[...]
    for s in range(slots):
        def keep(s=s):
            land_ref[g, s, me] = stage_ref[head_of(s, me, ranks)]

        pl.when(known(s, me))(keep)
        for which in range(groups - 1):
            def clear(s=s, which=which):
                land_ref[which, s] = jnp.zeros(land_ref.shape[2:], BF)

            pl.when(head_of(s, me, ranks) >= heads)(clear)
    gx_ref[me] = x_ref[...]
    gc_ref[me, :, :width] = c_ref[...]
    routes = id_ref[...].astype(F32).astype(BF)
    blank = jnp.zeros((routes.shape[0], LANES - routes.shape[1]), BF)
    gc_ref[me, :, width:] = jnp.concatenate([routes, blank], -1)

    def share(s, part, d, to):
        return remote(part, part, d_send.at[s, d], d_recv.at[s, d], dp=to)

    def pass_on(i):
        for s in range(slots):
            part = land_ref.at[g, s, i]
            for d in range(1, groups):
                pl.when(known(s, me))(lambda: share(s, part, d, peers[d - 1]).start())

    def out_share(d, k, group):
        part = half_ref.at[group, k]
        return remote(part, part, p_send.at[d, k], p_recv.at[d, k], dp=peers[d - 1])

    def held(group, k):
        return True if (groups - 1) * per + k < units else group * per + k < units

    pass_on(me)
    for d in range(1, ranks):
        i = lax.rem(me + ranks - d, ranks)
        for s in range(slots):
            pl.when(known(s, me))(lambda: weight_copy(s, d, 0, i, others[0]).wait_recv())
        pass_on(i)
    steps = ranks // 2 - 1
    for step in range(1, steps + 1):
        out_rows.step(step)
        if step == 1:
            tokens.step(1)
    out_rows.finish()
    for d in range(1, groups):
        for k in range(per):
            guarded(held(g, k), out_share(d, k, g).start)
    cots = LineGather(ranks, gc_ref.at[me], lambda i: gc_ref.at[i], c_send, c_recv)
    for step in range(2, steps + 1):
        tokens.step(step)
        if step == steps - 1:
            cots.start()
    if steps < 3:
        cots.start()
    tokens.finish()
    for d in range(1, groups):
        there = lax.rem(g + groups - d, groups)
        for s in range(slots):
            pl.when(known(s, me, there))(lambda: share(s, land_ref.at[there, s], d, peers[d - 1]).wait_recv())
    for which, ref in enumerate((wqs_ref, wks_ref, wvs_ref, wps_ref)):
        for s in range(slots):
            for r in range(ranks):
                ref[r * rows : (r + 1) * rows, s * LANES : (s + 1) * LANES] = land_ref[which, s, r]
    small_ref[...] = jnp.transpose(wps_ref[:, (slots - 1) * LANES :].astype(F32))
    attend(
        seqs, slots, gain_at, gx_ref, small_ref, wqs_ref, wks_ref, wvs_ref, cos_ref, sin_ref,
        inv_ref, q_ref, k_ref, v_ref, mixed_ref, lse_ref,
        [functools.partial(cots.step, step) for step in range(1, steps + 1)],
    )
    cots.finish()
    for d in range(1, ranks):
        t = others[d - 1]
        for s in range(slots):
            pl.when(known(s, t))(lambda: weight_copy(s, d, 0, me, t).wait_send())
    for d in range(1, groups):
        there = lax.rem(g + groups - d, groups)
        for s in range(slots):
            pl.when(known(s, me))(lambda: share(s, land_ref.at[g, s], d, peers[d - 1]).wait_send())
        for k in range(per):
            guarded(held(g, k), out_share(d, k, g).wait_send)
            guarded(held(there, k), out_share(d, k, there).wait_recv)


def front(
    ranks, groups, heads, seqs, slots, gain_at, x, cot, ids, w_query, w_key, w_value, s_gate, s_up, rest, w_output,
    cosine, sine,
):
    own, width = x.shape
    total, span = ranks * own, slots * LANES
    rows = w_query.shape[0]
    per = -(-(width // LANES) // groups)
    line = LineGather.semaphores(ranks)
    dma = pltpu.SemaphoreType.DMA
    spec = pl.BlockSpec(memory_space=pltpu.VMEM)
    shape = jax.ShapeDtypeStruct
    return pl.pallas_call(
        functools.partial(front_kernel, ranks, groups, heads, seqs, slots, gain_at),
        out_shape=[shape((ranks, own, width), BF), shape((ranks, own, width + LANES), BF)]
        + [shape((width, slots * LANES), BF)] * 4
        + [shape((LANES, width), F32), shape((groups, per, ranks // 2, rows, LANES), BF)]
        + [shape((total, 1), F32)]
        + [shape((total, span), BF)] * 4
        + [shape((total, slots), F32)],
        in_specs=[spec] * 12,
        out_specs=[spec] * 14,
        scratch_shapes=[
            pltpu.VMEM((slots * ranks, rows, LANES), BF),
            pltpu.VMEM((groups, slots, ranks, rows, LANES), BF),
            pltpu.VMEM((per, rows, LANES), BF),
            dma((line,)), dma((line,)),
            dma((line,)), dma((line,)),
            dma((slots, ranks)), dma((slots, ranks)),
            dma((slots, groups)), dma((slots, groups)),
            dma((line,)), dma((line,)),
            dma((groups, per)), dma((groups, per)),
        ],
        compiler_params=pltpu.CompilerParams(
            collective_id=0, has_side_effects=True, vmem_limit_bytes=VMEM_LIMIT
        ),
        name="front",
    )(x, cot, ids, w_query, w_key, w_value, s_gate, s_up, rest, w_output, cosine, sine)


def project_kernel(
    ranks, groups, heads, slots, count, top, route_at,
    x_ref, mixed_ref, half_ref, small_ref, pack_ref, c_ref,
    resid_ref, n_ref, all_ref, wo_ref, packed_ref, turned_ref, c_all_ref, other_ref, id_ref,
    send, recv, t_send, t_recv, a_send, a_recv, load,
):
    me, g = lax.axis_index("expert"), lax.axis_index("dp")
    chips = ranks // 2
    z = me // 2
    twin = me + 1 - 2 * lax.rem(me, 2)
    per, part = half_ref.shape[1], half_ref.shape[3]
    units = wo_ref.shape[1] // LANES
    peers = [lax.rem(g + d, groups) for d in range(1, groups)]
    lanes = c_all_ref.shape[-1]
    across = Across(lambda r: c_ref.at[r, pl.ds(0, lanes)], c_all_ref, a_send, a_recv)
    meet_near(chips, z, me, peers)
    ids = pltpu.make_async_copy(c_ref.at[:, pl.ds(wo_ref.shape[1], LANES)], id_ref, load)
    ids.start()
    line = LineGather.semaphores(ranks)
    parts = []
    for s in range(slots):
        def head(i, s=s):
            return aligned(jnp.clip(head_of(s, i, ranks), 0, heads - 1), LANES)

        cols = slice(s * LANES, (s + 1) * LANES)
        ok = (lambda i: True) if (s + 1) * ranks <= heads else (lambda i, s=s: head_of(s, i, ranks) < heads)
        gather = LineGather(
            ranks, mixed_ref.at[:, cols], lambda i, head=head: all_ref.at[:, head(i)], send, recv, s * line, ok
        )
        gather.start()
        parts.append(gather)

    across.start()
    across.more()
    for s, gather in enumerate(parts):
        def keep(s=s):
            cols = slice(s * LANES, (s + 1) * LANES)
            all_ref[:, aligned(jnp.clip(head_of(s, me, ranks), 0, heads - 1), LANES)] = mixed_ref[:, cols]

        guarded(gather.valid(me), keep)

    def share_twin(group, k):
        src = half_ref.at[group, k]
        return remote(src, other_ref.at[group, k], t_send.at[group, k], t_recv.at[group, k], expert=twin)

    def each_unit(action):
        for group in range(groups):
            for k in range(per):
                if group * per + k < units:
                    action(share_twin(group, k))

    each_unit(lambda copy: copy.start())
    middle = (chips + 1) // 2
    for step in range(1, chips):
        for gather in parts:
            gather.step(step)
        if step == middle:
            across.relay()
    for gather in parts:
        gather.finish()
    each_unit(lambda copy: copy.wait())
    ids.wait()

    def lay_out(even, odd):
        for u in range(units):
            cols = slice(u * LANES, (u + 1) * LANES)
            for c in range(chips):
                wo_ref[2 * c * part : (2 * c + 1) * part, cols] = even[u // per, u % per, c]
                wo_ref[(2 * c + 1) * part : (2 * c + 2) * part, cols] = odd[u // per, u % per, c]

    pl.when(me == 2 * z)(lambda: lay_out(half_ref, other_ref))
    pl.when(me != 2 * z)(lambda: lay_out(other_ref, half_ref))
    blocks, own, width = x_ref.shape
    names = ranks * count
    gain_at = route_at + names + 1 - (slots - 1) * LANES
    gain = small_ref[gain_at : gain_at + 1, :]
    tile = 2 if own <= 128 and blocks % 2 == 0 else 1

    def rows_of(b):
        rows = aligned(b, tile * own)
        x = x_ref[pl.ds(b * tile, tile)].reshape(tile * own, width).astype(F32)
        resid = x + dot(all_ref[rows, :], wo_ref[...])
        inverse = lax.rsqrt(jnp.mean(resid * resid, -1, keepdims=True) + EPS)
        normed = (resid * inverse * gain).astype(BF)
        n_ref[rows, :] = normed
        for t in range(tile):
            def keep(t=t):
                resid_ref[...] = resid[t * own : (t + 1) * own]

            pl.when(b * tile + t == me)(keep)
        probs = route_probs(dot(normed, pack_ref[...]), route_at, names)
        routes = id_ref[rows, :].astype(jnp.int32)
        lane = lax.broadcasted_iota(jnp.int32, routes.shape, 1)
        out = jnp.zeros((tile * own, LANES), F32)
        for j in range(count):
            mine = me * count + j
            chosen = jnp.max(jnp.where((routes == mine) & (lane < top), 1.0, 0.0), -1, keepdims=True)
            names_at = lax.broadcasted_iota(jnp.int32, probs.shape, 1)
            weight = chosen * jnp.sum(jnp.where(names_at == mine, probs, 0.0), -1, keepdims=True)
            high = weight.astype(BF).astype(F32)
            out = jnp.where(lane == j, high, out)
            out = jnp.where(lane == count + j, weight - high, out)
        packed_ref[rows, :] = out.astype(BF)
        turned_ref[:, rows] = jnp.transpose(out)[:turned_ref.shape[0]].astype(BF)

    half = blocks // tile // 2
    lax.fori_loop(0, half, lambda b, c: (rows_of(b), c)[1], 0)
    across.hand_over()
    lax.fori_loop(half, blocks // tile, lambda b, c: (rows_of(b), c)[1], 0)
    across.finish()


def route_probs(products, first, names):
    logits = products[:, first : first + names]
    raised = jnp.exp(logits - jnp.max(logits, -1, keepdims=True))
    return raised / jnp.sum(raised, -1, keepdims=True)


def project(ranks, groups, heads, slots, count, top, route_at, lanes, x, mixed, half, small, pack, cot):
    blocks, own, width = x.shape
    total = blocks * own
    line = LineGather.semaphores(ranks)
    per = half.shape[1]
    dma = pltpu.SemaphoreType.DMA
    spec = pl.BlockSpec(memory_space=pltpu.VMEM)
    anywhere = pl.BlockSpec(memory_space=pl.ANY)
    shape = jax.ShapeDtypeStruct
    return pl.pallas_call(
        functools.partial(project_kernel, ranks, groups, heads, slots, count, top, route_at),
        out_shape=[
            shape((own, width), F32),
            shape((total, width), BF),
            shape((total, width), BF),
            shape((width, width), BF),
            shape((total, LANES), BF),
            shape((TURNED, total), BF),
            shape((6, total // 2, lanes), BF),
        ],
        in_specs=[spec] * 5 + [anywhere],
        out_specs=[spec] * 6 + [anywhere],
        scratch_shapes=[
            pltpu.VMEM(half.shape, BF), pltpu.VMEM((total, LANES), BF),
            dma((slots * line,)), dma((slots * line,)),
            dma((groups, per)), dma((groups, per)),
            dma((Across.SEMAPHORES,)), dma((Across.SEMAPHORES,)), dma(()),
        ],
        compiler_params=pltpu.CompilerParams(
            collective_id=1, has_side_effects=True, vmem_limit_bytes=VMEM_LIMIT
        ),
        name="project",
    )(x, mixed, half, small, pack, cot)


def attend(
    seqs, slots, gain_at, x_ref, small_ref, wq_ref, wk_ref, wv_ref, cos_ref, sin_ref,
    inv_ref, q_ref, k_ref, v_ref, mixed_ref, lse_ref, hooks,
):
    ranks, own, width = x_ref.shape
    pos = own // seqs
    length = ranks * pos
    block = row_block(length)
    count = block // pos
    scale = HEAD_DIM ** (-0.5)
    gain = small_ref[gain_at : gain_at + 1, :]
    hooks = list(hooks)

    def progress():
        if hooks:
            hooks.pop(0)()

    for s in range(seqs):
        for i in range(length // block):
            rows = pl.ds(s * length + i * block, block)
            x = [x_ref[e, s * pos : (s + 1) * pos, :] for e in range(i * count, (i + 1) * count)]
            x = jnp.concatenate(x, 0).astype(F32)
            inv = lax.rsqrt(jnp.mean(x * x, -1, keepdims=True) + EPS)
            normed = (x * inv * gain).astype(BF)
            inv_ref[rows, :] = inv
            cosine = cos_ref[pl.ds(i * block, block), :]
            sine = sin_ref[pl.ds(i * block, block), :]
            queries, keyed, valued = dot(normed, wq_ref[...]), dot(normed, wk_ref[...]), dot(normed, wv_ref[...])
            for h in range(slots):
                cols = slice(h * HEAD_DIM, (h + 1) * HEAD_DIM)
                q, k = queries[:, cols], keyed[:, cols]
                q_ref[rows, cols] = (q * cosine + pltpu.roll(q, HEAD_DIM // 2, 1) * sine).astype(BF)
                k_ref[rows, cols] = (k * cosine + pltpu.roll(k, HEAD_DIM // 2, 1) * sine).astype(BF)
            v_ref[rows, :] = valued.astype(BF)
    progress()
    for s in range(seqs):
        for i in range(length // block):
            if i:
                progress()
            rows = pl.ds(s * length + i * block, block)
            keys = pl.ds(s * length, (i + 1) * block)
            shape = (block, (i + 1) * block)
            seen = (
                lax.broadcasted_iota(jnp.int32, shape, 1)
                <= lax.broadcasted_iota(jnp.int32, shape, 0) + i * block
            )
            for h in range(slots):
                cols = slice(h * HEAD_DIM, (h + 1) * HEAD_DIM)
                scores = dot_nt(q_ref[rows, cols], k_ref[keys, cols]) * scale
                scores = jnp.where(seen, scores, MASKED)
                top = jnp.max(scores, -1, keepdims=True)
                raised = jnp.exp(scores - top)
                totals = jnp.sum(raised, -1, keepdims=True)
                probs = (raised / totals).astype(BF)
                mixed_ref[rows, cols] = dot(probs, v_ref[keys, cols]).astype(BF)
                lse_ref[rows, h : h + 1] = top + jnp.log(totals)
    while hooks:
        progress()


def attend_back_kernel(
    ranks, heads, seqs, slots, gain_at, da_ref, x_ref, inv_ref, small_ref, wq_ref, wk_ref, wv_ref, wall_ref,
    cos_ref, sin_ref,
    q_ref, k_ref, v_ref, lse_ref,
    dn_ref, dwq_ref, dwk_ref, dwv_ref, gain_ref, dmix_ref, dqkv_ref, dk_ref, dv_ref, wo_ref,
):
    total, width = da_ref.shape
    length = total // seqs
    block = row_block(length)
    count = length // block
    scale = HEAD_DIM ** (-0.5)
    span = slots * HEAD_DIM
    me = lax.axis_index("expert")
    for h in range(slots):
        cols = slice(h * HEAD_DIM, (h + 1) * HEAD_DIM)
        head = head_of(h, me, ranks)
        rows_here = wall_ref[aligned(jnp.minimum(head, heads - 1), HEAD_DIM), :]
        wo_ref[cols, :] = jnp.where(head < heads, rows_here, jnp.zeros_like(rows_here))
    for s in range(seqs):
        for i in range(count):
            rows = pl.ds(s * length + i * block, block)
            dmix_ref[rows, :] = dot_nt(da_ref[rows, :], wo_ref[...]).astype(BF)
        for h in range(slots):
            cols = slice(h * HEAD_DIM, (h + 1) * HEAD_DIM)
            dk_ref[...] = jnp.zeros_like(dk_ref)
            dv_ref[...] = jnp.zeros_like(dv_ref)
            for i in range(count):
                rows = pl.ds(s * length + i * block, block)
                reach = (i + 1) * block
                keys = pl.ds(s * length, reach)
                shape = (block, reach)
                seen = (
                    lax.broadcasted_iota(jnp.int32, shape, 1)
                    <= lax.broadcasted_iota(jnp.int32, shape, 0) + i * block
                )
                q = q_ref[rows, cols]
                k = k_ref[keys, cols]
                dmix = dmix_ref[rows, cols]
                scores = jnp.where(seen, dot_nt(q, k) * scale, MASKED)
                probs = jnp.exp(scores - lse_ref[rows, h : h + 1])
                dp = dot_nt(dmix, v_ref[keys, cols])
                delta = jnp.sum(probs * dp, -1, keepdims=True)
                ds = (probs * (dp - delta)).astype(BF)
                dq = dot(ds, k) * scale
                cosine = cos_ref[pl.ds(i * block, block), :]
                sine = sin_ref[pl.ds(i * block, block), :]
                dqkv_ref[rows, h * HEAD_DIM : (h + 1) * HEAD_DIM] = (
                    dq * cosine - pltpu.roll(dq, HEAD_DIM // 2, 1) * sine
                ).astype(BF)
                dk_ref[pl.ds(0, reach), :] += dot_tn(ds, q)
                dv_ref[pl.ds(0, reach), :] += dot_tn(probs.astype(BF), dmix)
            for i in range(count):
                rows = pl.ds(s * length + i * block, block)
                here = pl.ds(i * block, block)
                dk = dk_ref[here, :] * scale
                dk = dk * cos_ref[here, :] - pltpu.roll(dk, HEAD_DIM // 2, 1) * sin_ref[here, :]
                dqkv_ref[rows, span + h * HEAD_DIM : span + (h + 1) * HEAD_DIM] = dk.astype(BF)
                dqkv_ref[rows, 2 * span + h * HEAD_DIM : 2 * span + (h + 1) * HEAD_DIM] = dv_ref[here, :].astype(BF)
    gain = jnp.zeros((1, width), F32)
    for i in range(total // block):
        rows = pl.ds(i * block, block)
        d_normed = dot_nt(dqkv_ref[rows, :span], wq_ref[...])
        d_normed += dot_nt(dqkv_ref[rows, span : 2 * span], wk_ref[...])
        d_normed += dot_nt(dqkv_ref[rows, 2 * span :], wv_ref[...])
        dn_ref[rows, :] = d_normed.astype(BF)
        gain += jnp.sum(d_normed * x_ref[rows, :].astype(F32) * inv_ref[rows, :], 0, keepdims=True)
    gain_ref[...] = gain
    step = LANES * 2
    for i in range(width // step):
        cols = slice(i * step, (i + 1) * step)
        normed = (x_ref[:, cols].astype(F32) * inv_ref[...] * small_ref[gain_at : gain_at + 1, cols]).astype(BF)
        grads = dot_tn(normed, dqkv_ref[...]).astype(BF)
        dwq_ref[cols, :] = grads[:, :span]
        dwk_ref[cols, :] = grads[:, span : 2 * span]
        dwv_ref[cols, :] = grads[:, 2 * span :]


def attend_back(ranks, heads, seqs, slots, gain_at, d_att, x, inverse, small, w_slices, w_all, cosine, sine, q, k, v, lse):
    total, width = d_att.shape
    span = slots * HEAD_DIM
    shape = jax.ShapeDtypeStruct
    return vmem_call(
        functools.partial(attend_back_kernel, ranks, heads, seqs, slots, gain_at),
        [shape((total, width), BF)] + [shape((width, span), BF)] * 3 + [shape((1, width), F32)],
        d_att, x, inverse, small, *w_slices, w_all, cosine, sine, q, k, v, lse,
        scratch_shapes=[
            pltpu.VMEM((total, span), BF),
            pltpu.VMEM((total, 3 * span), BF),
            pltpu.VMEM((total // seqs, HEAD_DIM), F32),
            pltpu.VMEM((total // seqs, HEAD_DIM), F32),
            pltpu.VMEM((span, width), BF),
        ],
        name="attend_back",
    )


def experts_kernel(
    ranks, count, steps, share, n_ref, c_ref, packed_ref, wg_ref, wu_ref, wd_ref, pack_ref, sd_ref,
    n_group, c_group, w_group,
    out_ref, dx_ref, dpack_ref, dsd_ref, n_all, c_all, w_all, og_ref, ou_ref, od_ref, send, recv,
):
    step = pl.program_id(0)
    me = lax.axis_index("expert")
    names = ranks * count
    part = c_all.shape[-1]
    moves = [
        SameExperts(w_group, w_all, send.at[1], recv.at[1]),
        Across(lambda r: n_group.at[r], n_all, send.at[0], recv.at[0]),
        Across(lambda r: c_group.at[r, pl.ds(n_ref.shape[1] - part, part)], c_all, send.at[2], recv.at[2]),
    ]

    @pl.when(step == 0)
    def _():
        meet(moves[0].peers() + moves[1].peers())
        for move in moves:
            move.start()

    @pl.when(step == min(1, steps - 1))
    def _():
        for move in moves:
            move.more()

    @pl.when(step == steps // 2)
    def _():
        for move in moves:
            move.relay()

    @pl.when(step == steps - 1)
    def _():
        for move in moves:
            move.hand_over()

    n = n_ref[...]
    c_b = c_ref[...]
    c = c_b.astype(F32)
    products = dot(n, pack_ref[...])
    gate, up = products[:, :share], products[:, share : 2 * share]
    hidden = (silu(gate) * up).astype(BF)
    out = dot(hidden, sd_ref[...])
    d_gate_s, d_up_s = swiglu_back(dot_nt(c_b, sd_ref[...]), gate, up)

    @pl.when(step == 0)
    def _():
        for ref in (dpack_ref, dsd_ref, og_ref, ou_ref, od_ref):
            ref[...] = jnp.zeros_like(ref)

    dsd_ref[...] += dot_tn(hidden, c_b)
    probs = route_probs(products, 2 * share, names)
    name = lax.broadcasted_iota(jnp.int32, probs.shape, 1)
    d_log = jnp.zeros_like(probs)
    inner = jnp.zeros((n.shape[0], 1), F32)
    dx = jnp.zeros(c.shape, F32)
    for j in range(count):
        weight = packed_ref[:, j : j + 1].astype(F32) + packed_ref[:, count + j : count + j + 1].astype(F32)
        gate = dot(n, wg_ref[j])
        up = dot(n, wu_ref[j])
        hidden = (silu(gate) * up).astype(BF)
        y = dot(hidden, wd_ref[j]).astype(BF).astype(F32)
        out += weight * y
        d_weight = weight * jnp.sum(c * y, -1, keepdims=True)
        d_log += jnp.where(name == me * count + j, d_weight, 0.0)
        inner += d_weight
        d_y = (weight * c).astype(BF)
        d_gate, d_up = swiglu_back(dot_nt(d_y, wd_ref[j]), gate, up)
        dx += dot_nt(d_gate, wg_ref[j]) + dot_nt(d_up, wu_ref[j])
        if j == count - 1:
            og_ref[...] += dot_tn(n, d_gate)
            ou_ref[...] += dot_tn(n, d_up)
            od_ref[...] += dot_tn(hidden, d_y)
    d_log = (d_log - probs * inner).astype(BF)
    rest = jnp.zeros((n.shape[0], pack_ref.shape[1] - 2 * share - names), BF)
    d_products = jnp.concatenate([d_gate_s, d_up_s, d_log, rest], -1)
    dx += dot_nt(d_products, pack_ref[...])
    dpack_ref[...] += dot_tn(n, d_products)
    out_ref[...] = out.astype(BF)
    dx_ref[...] = dx.astype(BF)

    @pl.when(step == steps - 1)
    def _():
        for move in moves:
            move.finish()


def experts(ranks, lanes, normed, cot, packed, turned, w_gate, w_up, w_down, pack, s_down):
    total, width = normed.shape
    count, _, hidden = w_gate.shape
    tile = 256 if total % 256 == 0 else total
    steps = total // tile
    share = s_down.shape[0]
    anywhere = pl.BlockSpec(memory_space=pl.ANY)
    dma = pltpu.SemaphoreType.DMA

    def rows(cols):
        return pl.BlockSpec((tile, cols), lambda i: (i, 0))

    def whole(a):
        zeros = (0,) * a.ndim
        return pl.BlockSpec(a.shape, lambda i: zeros, pipeline_mode=pl.Buffered(1))

    shape = jax.ShapeDtypeStruct
    fixed = (w_gate, w_up, w_down, pack, s_down)
    flops = total * width * hidden * count * 12
    return pl.pallas_call(
        functools.partial(experts_kernel, ranks, count, steps, share),
        grid=(steps,),
        in_specs=[rows(width), rows(width), rows(LANES)] + [whole(a) for a in fixed] + [anywhere] * 3,
        out_specs=[
            rows(width),
            rows(width),
            pl.BlockSpec(pack.shape, lambda i: (0, 0)),
            pl.BlockSpec((share, width), lambda i: (0, 0)),
            anywhere, anywhere, anywhere,
            *(pl.BlockSpec(a.shape[1:], lambda i: (0, 0), pipeline_mode=pl.Buffered(1)) for a in fixed[:3]),
        ],
        out_shape=[
            shape((total, width), BF),
            shape((total, width), BF),
            shape(pack.shape, F32),
            shape((share, width), F32),
            shape((6, total // 2, width), BF),
            shape((6, total // 2, lanes), BF),
            shape((6, TURNED, total // 2), BF),
            *(shape(a.shape[1:], F32) for a in fixed[:3]),
        ],
        scratch_shapes=[dma((3, Across.SEMAPHORES)), dma((3, Across.SEMAPHORES))],
        compiler_params=pltpu.CompilerParams(
            vmem_limit_bytes=VMEM_LIMIT, collective_id=3, has_side_effects=True
        ),
        cost_estimate=pl.CostEstimate(flops=flops, bytes_accessed=30 * 2**20, transcendentals=0),
        name="experts",
    )(normed, cot, packed, *fixed, normed, cot, turned)


def weight_of(packed, j, count):
    return packed[:, j : j + 1].astype(F32) + packed[:, count + j : count + j + 1].astype(F32)


def routed_tile(n, c, weight, w_gate, w_up, w_down, acc_gate, acc_up, acc_down):
    d_y = jnp.concatenate([(weight * part.astype(F32)).astype(BF) for part in c], -1)
    gate, up = dot(n, w_gate), dot(n, w_up)
    d_gate, d_up = swiglu_back(dot_nt(d_y, w_down), gate, up)
    hidden = (silu(gate) * up).astype(BF)
    acc_gate[...] += dot_tn(n, d_gate)
    acc_up[...] += dot_tn(n, d_up)
    acc_down[...] += dot_tn(hidden, d_y)


def weights_kernel(
    j, count, first, size, own_steps, n_own, c_own, packed_own, n_ref, ca_ref, cb_ref, packed_ref,
    wg_ref, wu_ref, wd_ref, *refs,
):
    dg_ref, du_ref, dd_ref, wg, wu, wd, acc_gate, acc_up, acc_down, load, store = refs[-11:]
    step = pl.program_id(0)
    cols = pl.ds(first, size)

    @pl.when(step == 0)
    def _():
        copies = [
            pltpu.make_async_copy(wg_ref.at[j, :, cols], wg, load.at[0]),
            pltpu.make_async_copy(wu_ref.at[j, :, cols], wu, load.at[1]),
            pltpu.make_async_copy(wd_ref.at[j, cols], wd, load.at[2]),
        ]
        for copy in copies:
            copy.start()
        for acc in (acc_gate, acc_up, acc_down):
            acc[...] = jnp.zeros_like(acc)
        for copy in copies:
            copy.wait()

    ours = step < own_steps
    parts, at = [], 0
    for ref in (ca_ref, cb_ref):
        lanes = ref.shape[-1]
        parts.append(jnp.where(ours, c_own[:, at : at + lanes], ref[...]))
        at += lanes
    theirs = [jnp.transpose(packed_ref[k].astype(F32)) for k in range(packed_ref.shape[0])]
    theirs = weight_of(jnp.concatenate(theirs, 0), j, count)
    routed_tile(
        jnp.where(ours, n_own[...], n_ref[...]),
        parts,
        jnp.where(ours, weight_of(packed_own[...], j, count), theirs),
        wg[...], wu[...], wd[...], acc_gate, acc_up, acc_down,
    )

    @pl.when(step == pl.num_programs(0) - 1)
    def _():
        copies = [
            pltpu.make_async_copy(acc_gate, dg_ref.at[j, :, cols], store.at[0]),
            pltpu.make_async_copy(acc_up, du_ref.at[j, :, cols], store.at[1]),
            pltpu.make_async_copy(acc_down, dd_ref.at[j, cols], store.at[2]),
        ]
        for copy in copies:
            copy.start()
        for copy in copies:
            copy.wait()


def expert_weights(j, first, size, tokens, weights, grads=None):
    own, others = tokens
    width = own[0].shape[1]
    count = weights[0].shape[0]
    turned = others[-1]
    others = [a.reshape(-1, a.shape[-1]) for a in others[:-1]]
    tile = min(1024, own[0].shape[0])
    own_steps = own[0].shape[0] // tile
    steps = own_steps + others[0].shape[0] // tile

    def own_rows(a):
        return pl.BlockSpec((tile, a.shape[-1]), lambda i: (jnp.minimum(i, own_steps - 1), 0))

    def rows(a):
        return pl.BlockSpec((tile, a.shape[-1]), lambda i: (jnp.maximum(i - own_steps, 0), 0))

    half = turned.shape[-1]
    if tile >= half:
        turned_spec = pl.BlockSpec((tile // half, TURNED, half), lambda i: (jnp.maximum(i - own_steps, 0), 0, 0))
    else:
        def place(i):
            k = jnp.maximum(i - own_steps, 0)
            return k // (half // tile), 0, k % (half // tile)

        turned_spec = pl.BlockSpec((1, TURNED, tile), place)

    anywhere = pl.BlockSpec(memory_space=pl.ANY)
    dma = pltpu.SemaphoreType.DMA
    before = [] if grads is None else list(grads)
    return pl.pallas_call(
        functools.partial(weights_kernel, j, count, first, size, own_steps),
        grid=(steps,),
        in_specs=[own_rows(a) for a in own] + [rows(a) for a in others] + [turned_spec]
        + [anywhere] * (3 + len(before)),
        out_specs=[anywhere] * 3,
        out_shape=[jax.ShapeDtypeStruct(w.shape, F32) for w in weights],
        scratch_shapes=[
            pltpu.VMEM((width, size), BF), pltpu.VMEM((width, size), BF), pltpu.VMEM((size, width), BF),
            pltpu.VMEM((width, size), F32), pltpu.VMEM((width, size), F32), pltpu.VMEM((size, width), F32),
            dma((3,)), dma((3,)),
        ],
        input_output_aliases={} if grads is None else {10: 0, 11: 1, 12: 2},
        compiler_params=pltpu.CompilerParams(vmem_limit_bytes=VMEM_LIMIT),
        cost_estimate=pl.CostEstimate(
            flops=steps * tile * width * size * 12, bytes_accessed=40 * 2**20, transcendentals=0
        ),
        name="expert_weights",
    )(*own, *others, turned, *weights, *before)


class Scatter:
    def __init__(self, part, pair, far, stage, mine, theirs, sems):
        self.me = lax.axis_index("expert")
        self.chips = part.shape[0]
        self.z, self.c = self.me // 2, lax.rem(self.me, 2)
        self.part, self.pair, self.far = part, pair, far
        self.stage, self.mine, self.theirs = stage, mine, theirs
        self.send, self.recv, self.local = sems
        self.near = mine is None

    def swap(self):
        twin = self.me + 1 - 2 * self.c
        return remote(self.part.at[:, 1 - self.c], self.pair, self.send.at[0], self.recv.at[0], expert=twin)

    def own(self):
        return pltpu.make_async_copy(self.part.at[:, self.c], self.stage, self.local.at[0])

    def start(self):
        self.swap().start()
        if self.near:
            self.own().start()

    def hop(self, d):
        to, source = lax.rem(self.z + d, self.chips), lax.rem(self.z + self.chips - d, self.chips)
        out = remote(
            self.stage.at[to], self.far.at[self.z], self.send.at[d], self.recv.at[d], expert=2 * to + self.c
        )
        back = remote(
            self.stage.at[to], self.far.at[source], self.send.at[d], self.recv.at[d], expert=2 * to + self.c
        )
        return out, back

    def load(self, src, dst, k):
        copy = pltpu.make_async_copy(src, dst, self.local.at[k])
        copy.start()
        return copy

    def add_pairs(self):
        if self.near:
            self.own().wait()
        self.swap().wait_recv()

        def one(i, carry):
            if self.near:
                self.stage[i] = (self.stage[i].astype(F32) + self.pair[i].astype(F32)).astype(BF)
                return carry
            copies = [self.load(self.part.at[i, self.c], self.mine, 0), self.load(self.pair.at[i], self.theirs, 1)]
            for copy in copies:
                copy.wait()
            self.stage[i] = (self.mine[...].astype(F32) + self.theirs[...].astype(F32)).astype(BF)
            return carry

        lax.fori_loop(0, self.chips, one, 0)
        for d in range(1, self.chips):
            self.hop(d)[0].start()

    def total(self):
        acc = self.stage[self.z].astype(F32)
        for d in range(1, self.chips):
            self.hop(d)[1].wait_recv()
            source = lax.rem(self.z + self.chips - d, self.chips)
            if self.near:
                acc += self.far[source].astype(F32)
            else:
                self.load(self.far.at[source], self.mine, 0).wait()
                acc += self.mine[...].astype(F32)
        return acc

    def finish(self):
        self.swap().wait_send()
        for d in range(1, self.chips):
            self.hop(d)[0].wait_send()


def tail_kernel(
    ranks, groups, heads, slots, j, count,
    dn_ref, dwq_ref, dwk_ref, dwv_ref, dpack_ref,
    n_all, ca_all, cb_all, packed_all, wg_ref, wu_ref, wd_ref, og_ref, ou_ref, od_ref,
    dn_sum, all_ref, dg_ref, du_ref, dd_ref, *refs,
):
    if dn_ref.shape[0] > 4:
        pair, far, mine, theirs = refs[:2] + refs[-2:]
        refs = refs[2:-2]
    else:
        pair, far = refs[-2:]
        mine = theirs = None
        refs = refs[:-2]
    (
        n_buf, c_buf, p_buf, wg, wu, wd, acc_gate, acc_up, acc_down, got_ref, sum_ref, stage,
        a_send, a_recv, a_local, r_send, r_recv, t_send, t_recv, g_send, g_recv, load, fetched,
    ) = refs
    me, g = lax.axis_index("expert"), lax.axis_index("dp")
    width = n_all.shape[2]
    rows = width // ranks
    tile = n_buf.shape[1]
    half = n_all.shape[1]
    per = half // tile
    steps = n_all.shape[0] * per
    parts, at = [], 0
    for ref in (ca_all, cb_all):
        parts.append(pl.ds(at, ref.shape[-1]))
        at += ref.shape[-1]
    peers = [lax.rem(g + d, groups) for d in range(1, groups)]
    others = [lax.rem(me + d, ranks) for d in range(1, ranks)]
    banks = (dwq_ref, dwk_ref, dwv_ref, dpack_ref)

    def tile_copies(sources, into):
        targets = (n_buf.at[into], p_buf.at[into], *(c_buf.at[into, :, part] for part in parts))
        return [
            pltpu.make_async_copy(src, dst, fetched.at[into, k]) for k, (src, dst) in enumerate(zip(sources, targets))
        ]

    def fetch(t, into):
        r = aligned(lax.rem(t, per), tile)
        sources = [n_all.at[t // per, r], packed_all.at[t // per, :, r], ca_all.at[t // per, r], cb_all.at[t // per, r]]
        for copy in tile_copies(sources, into):
            copy.start()

    fetch(0, 0)
    copies = [
        pltpu.make_async_copy(src, dst, load.at[k])
        for k, (src, dst) in enumerate((
            (wg_ref.at[j], wg), (wu_ref.at[j], wu), (wd_ref.at[j], wd),
            (og_ref, acc_gate), (ou_ref, acc_up), (od_ref, acc_down),
        ))
    ]
    for copy in copies:
        copy.start()
    meet([{"expert": t} for t in others] + [{"dp": t} for t in peers])
    first = Scatter(dn_ref, pair, far, stage, mine, theirs, (a_send, a_recv, a_local))
    first.start()

    def slot(s):
        return slice(s * LANES, (s + 1) * LANES)

    def has(s, i, group):
        return jnp.logical_or(group == groups - 1, head_of(s, i, ranks) < heads)

    def reduce_copy(d, s, which):
        return remote(
            banks[which].at[:, slot(s)], got_ref.at[d - 1, :, slot(s)], r_send.at[d, s], r_recv.at[d, s], dp=peers[d - 1]
        )

    for d in range(1, groups):
        for s in range(slots):
            for which in range(groups):
                ok = jnp.logical_and(peers[d - 1] == which, has(s, me, which))
                pl.when(ok)(lambda: reduce_copy(d, s, which).start())

    for copy in copies:
        copy.wait()

    def turn_copy(d, s, i, to):
        return remote(
            sum_ref.at[to, :, slot(s)], all_ref.at[g, i, :, slot(s)], t_send.at[d, s], t_recv.at[d, s], expert=to
        )

    def add_groups():
        for s in range(slots):
            def one(s=s):
                for d in range(1, groups):
                    reduce_copy(d, s, 0).wait_recv()
                for which in range(groups):
                    def add(which=which):
                        for r in range(ranks):
                            here = slice(r * rows, (r + 1) * rows)
                            acc = banks[which][here, slot(s)].astype(F32)
                            for d in range(1, groups):
                                acc += got_ref[d - 1, here, slot(s)].astype(F32)
                            sum_ref[r, :, slot(s)] = acc.astype(BF)

                    pl.when(g == which)(add)
                all_ref[g, me, :, slot(s)] = sum_ref[me, :, slot(s)]
                for d in range(1, ranks):
                    turn_copy(d, s, me, others[d - 1]).start()

            pl.when(has(s, me, g))(one)

    by_x = g + 1 - 2 * lax.rem(g, 2)
    by_y = lax.rem(g + 2, 4)
    by_both = by_y + 1 - 2 * lax.rem(by_y, 2)

    def pieces(group, h):
        mid = ranks // 2
        found = []
        for s in range(slots):
            part = all_ref.at[group, pl.ds(h * mid, mid), :, slot(s)]
            if (s + 1) * ranks <= heads:
                found.append((True, part))
                continue
            found.append((group == groups - 1, part))
            present = [i for i in range(ranks) if head_of(s, i, ranks) < heads]
            for i in present[h::2]:
                found.append((group != groups - 1, all_ref.at[group, i, :, slot(s)]))
        return found

    def spread(k, group, h, to):
        copies = []
        for n, (ok, part) in enumerate(pieces(group, h)):
            at = (k * 2 + h) * ranks + n
            copies.append((ok, remote(part, part, g_send.at[at], g_recv.at[at], dp=to)))
        return copies

    def act(copies, what):
        for ok, copy in copies:
            guarded(ok, getattr(copy, what))

    def spread_out():
        for d in range(1, ranks):
            i = lax.rem(me + ranks - d, ranks)
            for s in range(slots):
                pl.when(has(s, i, g))(lambda: turn_copy(d, s, i, others[0]).wait_recv())
        for k, h, to in ((0, 0, by_x), (1, 1, by_y), (0, 1, by_x), (1, 0, by_y)):
            act(spread(k, g, h, to), "start")

    def pass_on():
        act(spread(0, by_x, 0, by_x), "wait_recv")
        act(spread(2, by_x, 0, by_y), "start")
        act(spread(1, by_y, 1, by_y), "wait_recv")
        act(spread(3, by_y, 1, by_x), "start")

    def keep_first():
        dn_sum[...] = first.total()

    first.add_pairs()
    hooks = [None, add_groups, None, spread_out, pass_on, keep_first]

    def step(t, carry):
        now = lax.rem(t, 2)
        pl.when(t + 1 < steps)(lambda: fetch(t + 1, 1 - now))
        r = pl.ds(0, tile)
        for copy in tile_copies([n_all.at[0, r], packed_all.at[0, :, r], ca_all.at[0, r], cb_all.at[0, r]], now):
            copy.wait()
        routed_tile(
            n_buf[now], [c_buf[now]], weight_of(jnp.transpose(p_buf[now].astype(F32)), j, count),
            wg[...], wu[...], wd[...], acc_gate, acc_up, acc_down,
        )
        for k, hook in enumerate(hooks):
            if hook is not None:
                pl.when(t == k * steps // len(hooks))(hook)
        return carry

    lax.fori_loop(0, steps, step, 0)
    stores = []
    for k, (acc, out) in enumerate(((acc_gate, dg_ref), (acc_up, du_ref), (acc_down, dd_ref))):
        half_size = (wg, wu, wd)[k]
        half_size[...] = acc[...].astype(BF)
        stores.append(pltpu.make_async_copy(half_size, out, load.at[k]))
        stores[-1].start()
    first.finish()
    for d in range(1, groups):
        for s in range(slots):
            pl.when(has(s, me, peers[d - 1]))(lambda: reduce_copy(d, s, 0).wait_send())
    act(spread(0, by_x, 1, by_x), "wait_recv")
    act(spread(1, by_y, 0, by_y), "wait_recv")
    act(spread(2, by_both, 0, by_y), "wait_recv")
    act(spread(3, by_both, 1, by_x), "wait_recv")
    for k, h, to in ((0, 0, by_x), (1, 1, by_y), (0, 1, by_x), (1, 0, by_y)):
        act(spread(k, g, h, to), "wait_send")
    act(spread(2, by_x, 0, by_y), "wait_send")
    act(spread(3, by_y, 1, by_x), "wait_send")
    for d in range(1, ranks):
        for s in range(slots):
            pl.when(has(s, me, g))(lambda: turn_copy(d, s, me, others[d - 1]).wait_send())
    for copy in stores:
        copy.wait()


def tail(ranks, groups, heads, slots, j, d_normed, d_weights, others, weights, own_grads):
    half, width = others[0].shape[1:]
    count, _, hidden = weights[0].shape
    chips = ranks // 2
    total = d_normed.shape[0]
    own = total // ranks
    rows = width // ranks
    span = slots * LANES
    tile = min(512, half)
    dma = pltpu.SemaphoreType.DMA
    shape = jax.ShapeDtypeStruct
    vmem, anywhere = pl.BlockSpec(memory_space=pltpu.VMEM), pl.BlockSpec(memory_space=pl.ANY)
    block = shape((chips, own, width), BF)
    near = chips <= 4
    return pl.pallas_call(
        functools.partial(tail_kernel, ranks, groups, heads, slots, j, count),
        out_shape=[
            shape((own, width), F32), shape((groups, ranks, rows, span), BF),
            shape((width, hidden), BF), shape((width, hidden), BF), shape((hidden, width), BF),
        ]
        + [block] * (0 if near else 2),
        in_specs=[anywhere] + [vmem] * 4 + [anywhere] * 10,
        out_specs=[vmem] * 2 + [anywhere] * (3 if near else 5),
        scratch_shapes=[
            pltpu.VMEM((2, tile, width), BF), pltpu.VMEM((2, tile, width), BF), pltpu.VMEM((2, TURNED, tile), BF),
            pltpu.VMEM((width, hidden), BF), pltpu.VMEM((width, hidden), BF), pltpu.VMEM((hidden, width), BF),
            pltpu.VMEM((width, hidden), F32), pltpu.VMEM((width, hidden), F32), pltpu.VMEM((hidden, width), F32),
            pltpu.VMEM((groups - 1, width, span), BF), pltpu.VMEM((ranks, rows, span), BF),
            pltpu.VMEM((chips, own, width), BF),
            dma((chips,)), dma((chips,)), dma((2,)),
            dma((groups, slots)), dma((groups, slots)),
            dma((ranks, slots)), dma((ranks, slots)),
            dma((8 * ranks,)), dma((8 * ranks,)),
            dma((6,)), dma((2, 4)),
        ]
        + ([pltpu.VMEM((chips, own, width), BF)] * 2 if near else [pltpu.VMEM((own, width), BF)] * 2),
        compiler_params=pltpu.CompilerParams(
            vmem_limit_bytes=VMEM_LIMIT, collective_id=4, has_side_effects=True
        ),
        cost_estimate=pl.CostEstimate(flops=total * groups * width * hidden * 12, bytes_accessed=2**26, transcendentals=0),
        name="tail",
    )(
        d_normed.reshape(chips, 2, own, width), *d_weights,
        *others, *weights, *own_grads,
    )[:5]


def outputs_kernel(
    heads, slots, j, gain_at, dn_ref, out_ref, resid_ref, dres_ref, x_ref, gain_ref, all_ref, wo_ref, sd_ref,
    eg_ref, eu_ref, ed_ref, bg_ref, bu_ref, bd_ref,
    layer_ref, dx_ref, q_ref, k_ref, v_ref, o_ref, sg_ref, su_ref, dsd_ref, small_ref, dg_ref, du_ref, dd_ref,
    hg, hu, hd, wide_g, wide_u, wide_d, load, store,
):
    loads = [
        pltpu.make_async_copy(src, dst, load.at[k])
        for k, (src, dst) in enumerate(((eg_ref, hg), (eu_ref, hu), (ed_ref, hd)))
    ]
    for copy in loads:
        copy.start()
    copies = []
    for k, (src, wide, dst) in enumerate(((hg, wide_g, dg_ref), (hu, wide_u, du_ref), (hd, wide_d, dd_ref))):
        loads[k].wait()
        wide[...] = src[...].astype(F32)
        copies.append(pltpu.make_async_copy(wide, dst.at[j], store.at[k]))
        copies[-1].start()
    layer_ref[...] = (resid_ref[...] + out_ref[...].astype(F32)).astype(BF)
    x = x_ref[...].astype(F32)
    inverse = lax.rsqrt(jnp.mean(x * x, -1, keepdims=True) + EPS)
    dx_ref[...] = (dres_ref[...] + norm_back(dn_ref[...], x, inverse, gain_ref[gain_at : gain_at + 1, :])).astype(BF)
    ranks = all_ref.shape[1]
    share = sg_ref.shape[1] // ranks
    for which, ref in enumerate((q_ref, k_ref, v_ref)):
        for h in range(heads):
            s, i = next((s, i) for s in range(slots) for i in range(ranks) if head_of(s, i, ranks) == h)
            ref[:, h * LANES : (h + 1) * LANES] = all_ref[which, i, :, s * LANES : (s + 1) * LANES].astype(F32)
    last = all_ref.shape[0] - 1
    small = jnp.zeros(small_ref.shape, F32)
    for i in range(ranks):
        here = all_ref[last, i].astype(F32)
        sg_ref[:, i * share : (i + 1) * share] = here[:, :share]
        su_ref[:, i * share : (i + 1) * share] = here[:, share : 2 * share]
        small += here
    small_ref[...] = small
    o_ref[...] = wo_ref[...].astype(F32)
    dsd_ref[...] = sd_ref[...].astype(F32)
    for copy in copies:
        copy.wait()


def outputs(heads, slots, j, gain_at, share_width, arrays, last_grads, grads):
    dn, out, resid, d_resid, x, gain, everything, d_wo, d_sd = arrays
    rows, span = everything.shape[2:]
    own, width = x.shape
    shape = jax.ShapeDtypeStruct
    vmem, anywhere = pl.BlockSpec(memory_space=pltpu.VMEM), pl.BlockSpec(memory_space=pl.ANY)
    return pl.pallas_call(
        functools.partial(outputs_kernel, heads, slots, j, gain_at),
        out_shape=[shape((own, width), BF)] * 2
        + [shape((rows, width), F32)] * 4
        + [shape((rows, share_width), F32)] * 2
        + [shape(d_sd.shape, F32), shape((rows, span), F32)]
        + [shape(a.shape, F32) for a in grads],
        in_specs=[vmem] * 9 + [anywhere] * 6,
        out_specs=[vmem] * 10 + [anywhere] * 3,
        scratch_shapes=[pltpu.VMEM(a.shape, BF) for a in last_grads]
        + [pltpu.VMEM(a.shape, F32) for a in last_grads]
        + [pltpu.SemaphoreType.DMA((3,)), pltpu.SemaphoreType.DMA((3,))],
        input_output_aliases={12: 10, 13: 11, 14: 12},
        compiler_params=pltpu.CompilerParams(vmem_limit_bytes=VMEM_LIMIT),
        name="outputs",
    )(*arrays, *last_grads, *grads)


def norm_back(grad, values, inverse, gain):
    scaled = grad * gain
    inner = jnp.mean(scaled * values, -1, keepdims=True)
    return inverse * scaled - values * inverse**3 * inner


def body(
    tokens, cotangent, attn_gain, ffn_gain, w_query, w_key, w_value, w_output, router,
    shared_gate, shared_up, shared_down, expert_gate, expert_up, expert_down, expert_ids,
):
    ranks = lax.axis_size("expert")
    me = lax.axis_index("expert")
    seqs, own_pos, width = tokens.shape
    length = own_pos * ranks
    total = seqs * length
    own = seqs * own_pos
    rows = w_query.shape[0]
    heads = width // HEAD_DIM
    slots = -(-heads // ranks)
    span = slots * HEAD_DIM
    share = shared_gate.shape[1] // ranks
    names = router.shape[1]
    count = expert_gate.shape[0]

    groups = lax.axis_size("dp")

    def in_order(a):
        return a.reshape(ranks, seqs, own_pos, -1).transpose(1, 0, 2, 3).reshape(total, -1)

    def by_rank(a):
        return a.reshape(seqs, ranks, own_pos, -1).transpose(1, 0, 2, 3).reshape(total, -1)

    rest = jnp.concatenate([router, attn_gain[:, None], ffn_gain[:, None]], -1)
    edges = [0, share, 2 * share, 2 * share + names, 2 * share + names + 1]
    gain_at = edges[3] - (slots - 1) * LANES
    top = expert_ids.shape[-1]
    cosine, sine = rotary_tables(length)
    (
        group_x, group_c, w_q, w_k, w_v, w_pack, small, half_out, inverse_one, q, k, v, mixed, lse,
    ) = front(
        ranks, groups, heads, seqs, slots, gain_at, tokens.reshape(own, width), cotangent.reshape(own, width),
        expert_ids.reshape(own, top), w_query, w_key, w_value, shared_gate, shared_up, rest, w_output,
        cosine, sine,
    )
    group_c = group_c.reshape(total, -1)
    gain_two = small[gain_at + 1 : gain_at + 2]
    units = width // LANES
    c_last = max(units // 5, 1) * LANES
    c_first = width - c_last
    resid, normed_two, all_mixed, all_out, packed, turned, all_ca = project(
        ranks, groups, heads, slots, count, top, edges[2], c_first, group_x, by_rank(mixed), half_out, small, w_pack, group_c
    )
    layer_part, d_normed_part, d_pack, d_s_down, all_n, all_cb, all_w, *own_grads = experts(
        ranks, c_last, normed_two, group_c, packed, turned, expert_gate, expert_up, expert_down, w_pack, shared_down
    )
    every = ((normed_two, group_c, packed), (all_n, all_ca, all_cb, all_w))
    banks = (expert_gate, expert_up, expert_down)
    hidden = expert_gate.shape[-1]
    cut = hidden * 4 // 7 if hidden % (7 * LANES) == 0 else hidden // 2

    def after(late, *earlier):
        return lax.optimization_barrier((late, earlier))[0]

    def scatter(partial):
        return lax.psum_scatter(partial, "expert", scatter_dimension=0, tiled=True)

    grads = expert_weights(0, 0, cut, every, banks)
    d_normed_two, grads = lax.optimization_barrier((scatter(d_normed_part), grads))
    d_normed_two = d_normed_two.astype(F32)
    inverse_two = lax.rsqrt(jnp.mean(resid * resid, -1, keepdims=True) + EPS)
    ffn_gain_part = jnp.sum(d_normed_two * resid * inverse_two, 0)
    d_out = cotangent.reshape(own, width).astype(F32)
    d_resid = d_out + norm_back(d_normed_two, resid, inverse_two, gain_two)
    own_att = d_resid.astype(BF)
    d_att = lax.all_gather(own_att, "expert", axis=0, tiled=True)
    grads = expert_weights(0, cut, hidden - cut, after(every, own_att), banks, grads)
    d_att, grads = lax.optimization_barrier((d_att, grads))

    d_normed_part, d_wq, d_wk, d_wv, attn_gain_part = attend_back(
        ranks, heads, seqs, slots, gain_at, in_order(d_att), in_order(group_x), inverse_one, small,
        (w_q, w_k, w_v), all_out, cosine, sine, q, k, v, lse
    )
    column = jnp.arange(span)[None, :]
    d_pack = jnp.where(column == edges[3], attn_gain_part.reshape(width, 1), d_pack)
    d_pack = jnp.where(column == edges[4], ffn_gain_part[:, None], d_pack).astype(BF)
    own_mixed = lax.dynamic_slice_in_dim(all_mixed, me * rows, rows, 1)
    d_wo_rows = dot_tn(own_mixed, d_att).astype(BF)
    d_wo_rows, d_sd_rows = lax.psum((d_wo_rows, d_s_down.astype(BF)), "dp")
    dn_sum, all_grads, *last_grads = tail(
        ranks, groups, heads, slots, 1, by_rank(d_normed_part), (d_wq, d_wk, d_wv, d_pack), every[1], banks, own_grads
    )
    layer_output, input_grad, g_q, g_k, g_v, g_o, g_sg, g_su, g_sd, small, g_gate, g_up, g_down = outputs(
        heads, slots, 1, gain_at, ranks * share,
        (dn_sum, scatter(after(layer_part, d_att)), resid, d_resid, tokens.reshape(own, width), small, all_grads, d_wo_rows, d_sd_rows),
        last_grads, grads,
    )
    g_r = small[:, edges[2] : edges[3]]
    g_one = small[:, edges[3]]
    g_two = small[:, edges[4]]
    return (
        layer_output.reshape(tokens.shape), input_grad.reshape(tokens.shape),
        g_one, g_two, g_q, g_k, g_v, g_o, g_r, g_sg, g_su, g_sd, g_gate, g_up, g_down,
    )


def solution(mesh):
    row = P("expert", None)
    experts_spec = P("expert", None, None)
    tokens_spec = P("dp", "expert", None)
    return jax.shard_map(
        body,
        mesh=mesh,
        in_specs=(tokens_spec, tokens_spec, P("expert"), P("expert"))
        + (row,) * 8
        + (experts_spec,) * 3
        + (P(("dp", "expert"), None, None),),
        out_specs=(tokens_spec, tokens_spec, P("expert"), P("expert")) + (row,) * 8 + (experts_spec,) * 3,
        check_vma=False,
    )
```

profile of v0, /device:TPU:13, one launch (start us, length us, event | category | flops | bytes accessed | tf_op | source)
XLA Modules:
  0.0 432.1 jit_solution(13969357908514093090)
XLA Ops:
  7.2 0.0 reduce-scatter.3.cloned.1.call-start
  7.2 0.7 broadcast_in_dim.38
  7.9 0.7 broadcast_in_dim.39
  8.5 0.7 pad_maximum_fusion
  9.2 0.7 copy.48.rest_ref
  10.0 1.4 copy.47
  11.4 72.1 %front.1 = (bf16[8,128,1280]{2,1,0:T(8,128)(2,1)}, bf16[8,128,1408]{2,1,0:T(8,128)(2,1)}, bf16[1280,256]{1,0:T(8,128)(2,1)}, bf16[1280,256]{1,0:T(8,128)(2,1)}, ...) custom-call(bf16[128,1280]{1,0:T(8,128)(2,1)} %bitcast.23, ...), custom_call_target="tpu_custom_call" | custom-call | tf_op jit(solution)/shard_map/front/pallas_call | solution.py:452
  83.6 55.1 %project.1 = (f32[128,1280]{1,0:T(8,128)}, bf16[1024,1280]{1,0:T(8,128)(2,1)}, bf16[1024,1280]{1,0:T(8,128)(2,1)}, bf16[1280,1280]{1,0:T(8,128)(2,1)}, bf16[1024...) custom-call(bf16[8,128,1280]{2,1,0:T(8,128)(2,1)} %get-tuple-element.91.x_ref, ...), custom_call_target="tpu_custom_call" | custom-call | tf_op jit(solution)/shard_map/project/pallas_call | solution.py:607
  138.6 71.0 %experts.1 = (bf16[1024,1280]{1,0:T(8,128)(2,1)}, bf16[1024,1280]{1,0:T(8,128)(2,1)}, f32[1280,256]{1,0:T(8,128)}, f32[112,1280]{1,0:T(8,128)}, bf16[6,512,1280]...) custom-call(bf16[1024,1280]{1,0:T(8,128)(2,1)} %get-tuple-element.11, ...), custom_call_target="tpu_custom_call" | custom-call | flops 28185722880 | bytes 31457280 | tf_op jit(solution)/shard_map/experts/pallas_call | solution.py:895
  209.6 0.0 copy-start
  209.6 0.0 reduce-scatter.3.cloned.1.call-update
  209.7 0.0 all-gather.2.cloned.1.call-start
  209.7 0.9 slice_reduce_fusion.2
  210.6 0.2 copy-done
  210.7 0.1 multiply_reduce_fusion
  210.9 0.0 copy-start.2
  210.9 42.1 %expert_weights.2 = (f32[2,1280,896]{2,1,0:T(8,128)}, f32[2,1280,896]{2,1,0:T(8,128)}, f32[2,896,1280]{2,1,0:T(8,128)}) custom-call(bf16[1024,1280]{1,0:T(8,128)(2,1)} %get-tuple-element.110.n_ref.n_group.n_own, bf16[1024,1408]{1,0:T(8,128)(2,1)} %bitcast.21, bf16[1024,128]{1,0:T(8,128)(2,1)} %get-tuple-element.112.packed_ref.packed_own, ...), custom_call_target="tpu_custom_call" | custom-call | flops 32212254720 | bytes 41943040 | tf_op jit(solution)/shard_map/expert_weights/pallas_call | solution.py:1019
  253.0 0.0 copy-start.3
  253.0 0.0 reduce-scatter.3.cloned.1.call-done
  253.0 1.3 fusion.6
  254.3 0.0 copy-done.2
  254.3 2.2 fusion.9
  256.5 0.0 all-gather.2.cloned.1.call-update
  256.5 0.0 all-reduce.3.cloned.1.call-start
  256.5 0.0 copy-done.3
  256.5 0.7 convert_element_type.23
  257.3 40.5 %expert_weights.3 = (f32[2,1280,896]{2,1,0:T(8,128)}, f32[2,1280,896]{2,1,0:T(8,128)}, f32[2,896,1280]{2,1,0:T(8,128)}) custom-call(bf16[1024,1280]{1,0:T(8,128)(2,1)} %get-tuple-element.110.n_ref.n_group.n_own, bf16[1024,1408]{1,0:T(8,128)(2,1)} %bitcast.22, ...), custom_call_target="tpu_custom_call", output_to_operand_aliasing={{0}: (10, {}), {1}: (11, {}), {2}: (12, {})} | custom-call | flops 24159191040 | bytes 41943040 | tf_op jit(solution)/shard_map/expert_weights/pallas_call | solution.py:1019
  297.8 0.0 all-gather.2.cloned.1.call-done.da_ref
  297.8 3.5 convolution_convert_fusion
  301.3 0.0 all-reduce.3.cloned.1.call-update
  301.4 0.3 reduce-scatter.5.cloned.1.call-start
  301.6 0.3 reduce-scatter.5.cloned.1.call-update
  301.9 0.0 copy-start.1
  302.0 18.3 %attend_back.1 = (bf16[1024,1280]{1,0:T(8,128)(2,1)}, bf16[1280,256]{1,0:T(8,128)(2,1)}, bf16[1280,256]{1,0:T(8,128)(2,1)}, bf16[1280,256]{1,0:T(8,128)(2,1)}, f32[1,1280]{1,0:T(1,128)}) custom-call(bf16[1024,1280]{1,0:T(8,128)(2,1)} %all-gather.2.cloned.1.call-done.da_ref, bf16[1024,1280]{1,0:T(8,128)(2,1)} %bitcast.17, ...), custom_call_target="tpu_custom_call" | custom-call | tf_op jit(solution)/shard_map/attend_back/pallas_call | solution.py:55
  320.2 0.7 reduce.1
  321.0 0.0 copy-done.1
  321.0 1.2 select_convert_fusion.dpack_ref
  322.2 87.0 %tail.1 = (f32[128,1280]{1,0:T(8,128)}, bf16[4,8,160,256]{3,2,1,0:T(8,128)(2,1)}, bf16[1280,896]{1,0:T(8,128)(2,1)}, bf16[1280,896]{1,0:T(8,128)(2,1)}, bf16[896,1280]{1,0:T(8,128)(2,1)}) custom-call(bf16[4,2,128,1280]{3,2,1,0:T(8,128)(2,1)} %bitcast.29, bf16[1280,256]{1,0:T(8,128)(2,1)} %get-tuple-element.134.dwq_ref, ...), custom_call_target="tpu_custom_call" | custom-call | flops 56371445760 | bytes 67108864 | tf_op jit(solution)/shard_map/tail/pallas_call | solution.py:1322
  409.2 0.0 all-reduce.3.cloned.1.call-done
  409.2 0.0 reduce-scatter.5.cloned.1.call-done.out_ref
  409.3 12.4 %outputs.1 = (bf16[128,1280]{1,0:T(8,128)(2,1)}, bf16[128,1280]{1,0:T(8,128)(2,1)}, f32[160,1280]{1,0:T(8,128)}, f32[160,1280]{1,0:T(8,128)}, f32[160,1280]{1,0:...) custom-call(f32[128,1280]{1,0:T(8,128)} %get-tuple-element.142.dn_re, ...), custom_call_target="tpu_custom_call", output_to_operand_aliasing={{10}: (12, {}), {11}: (13, {}), {12}: (14, {})} | custom-call | tf_op jit(solution)/shard_map/outputs/pallas_call | solution.py:1403
  421.7 1.8 slice_reduce_fusion
  423.5 1.0 slice.15
  424.4 0.7 copy.49
  (3 shorter events, 0.0 us)
Async XLA Ops:
  7.2 245.8 %reduce-scatter.3.cloned.1.call-start = ((), (), s32[]{:S(2)}) async-start(), calls=%async_computation.2 | async-start | bytes 2949120 | tf_op jit(solution)/shard_map/reduce_scatter | solution.py:1485
  209.6 1.1 copy-start
  209.7 88.2 %all-gather.2.cloned.1.call-start = ((), (), s32[]{:S(2)}) async-start(), calls=%async_computation.3 | async-start | bytes 2949120 | tf_op jit(solution)/shard_map/all_gather | solution.py:1495
  210.9 43.4 %copy-start.2 = (bf16[1,128,1280]{2,1,0:T(8,128)(2,1)S(1)}, bf16[1,128,1280]{2,1,0:T(8,128)(2,1)}, u32[]{:S(2)}) copy-start(bf16[1,128,1280]{2,1,0:T(8,128)(2,1)} %param.19) | copy-start | bytes 983044
  253.0 3.5 copy-start.3
  256.5 152.8 %all-reduce.3.cloned.1.call-start = ((), (), s32[]{:S(2)}) async-start(), calls=%async_computation.5 | async-start | bytes 1392640 | tf_op jit(solution)/shard_map/psum | solution.py:1508
  301.4 107.9 %reduce-scatter.5.cloned.1.call-start = ((), (), s32[]{:S(2)}) async-start(), calls=%async_computation.4 | async-start | bytes 2949120 | tf_op jit(solution)/shard_map/reduce_scatter | solution.py:1485
  301.9 19.0 %copy-start.1 = (f32[1280,256]{1,0:T(8,128)S(1)}, f32[1280,256]{1,0:T(8,128)}, u32[]{:S(2)}) copy-start(f32[1280,256]{1,0:T(8,128)} %get-tuple-element.138) | copy-start | bytes 3932164
Sparse Core Ops, SparseCore 0:
  209.8 33.8 reduce-scatter.2
  256.6 34.5 all-gather.1
  301.5 53.0 all-reduce.2
  356.9 41.5 reduce-scatter.4
where the time goes:
time: 440 us; the launch traced here: 432 us
  Pallas kernels  398 us (90%)
  between operations  14.4 us (3%)
  local copies, waits for them, and re-layouts  7.91 us (2%)
  other arithmetic  6.97 us (2%)
    pallas_call x1, Pallas kernels, tail(): pl.pallas_call(functools.partial(tail_kernel, ranks, groups, heads, slots...  87 us
    pallas_call x2, Pallas kernels, expert_weights(): pl.pallas_call(functools.partial(weights_kernel, j, count, first, size, o...  82.6 us
    pallas_call x1, Pallas kernels, front(): pl.pallas_call(functools.partial(front_kernel, ranks, groups, heads, seqs...  72.1 us
    pallas_call x1, Pallas kernels, experts(): pl.pallas_call(functools.partial(experts_kernel, ranks, count, steps, sha...  71 us
    pallas_call x1, Pallas kernels, project(): pl.pallas_call(functools.partial(project_kernel, ranks, groups, heads, sl...  55.1 us
    pallas_call x1, Pallas kernels, vmem_call(): pl.pallas_call(kernel, out_shape=outs, in_specs=[spec] * len(args), out_s...  18.3 us
    pallas_call x1, Pallas kernels, outputs(): pl.pallas_call(functools.partial(outputs_kernel, heads, slots, j, gain_at...  12.4 us
  transfers between devices with their start and end apart: 4, of which 0 were waited for; matrix products, arithmetic and copies ran while one was open for 1% of the time, Pallas kernels for 43%

commit v1 on v0

--- a/solution.py
+++ b/solution.py
@@ -529,26 +529,25 @@
                     action(share_twin(group, k))
 
     each_unit(lambda copy: copy.start())
+    def lay_out(even, odd):
+        for u in range(units):
+            cols = slice(u * LANES, (u + 1) * LANES)
+            for c in range(chips):
+                wo_ref[2 * c * part : (2 * c + 1) * part, cols] = even[u // per, u % per, c]
+                wo_ref[(2 * c + 1) * part : (2 * c + 2) * part, cols] = odd[u // per, u % per, c]
+
     middle = (chips + 1) // 2
     for step in range(1, chips):
         for gather in parts:
             gather.step(step)
         if step == middle:
             across.relay()
+            each_unit(lambda copy: copy.wait())
+            pl.when(me == 2 * z)(lambda: lay_out(half_ref, other_ref))
+            pl.when(me != 2 * z)(lambda: lay_out(other_ref, half_ref))
     for gather in parts:
         gather.finish()
-    each_unit(lambda copy: copy.wait())
     ids.wait()
-
-    def lay_out(even, odd):
-        for u in range(units):
-            cols = slice(u * LANES, (u + 1) * LANES)
-            for c in range(chips):
-                wo_ref[2 * c * part : (2 * c + 1) * part, cols] = even[u // per, u % per, c]
-                wo_ref[(2 * c + 1) * part : (2 * c + 2) * part, cols] = odd[u // per, u % per, c]
-
-    pl.when(me == 2 * z)(lambda: lay_out(half_ref, other_ref))
-    pl.when(me != 2 * z)(lambda: lay_out(other_ref, half_ref))
     blocks, own, width = x_ref.shape
     names = ranks * count
     gain_at = route_at + names + 1 - (slots - 1) * LANES
@@ -789,7 +788,8 @@
 def experts_kernel(
     ranks, count, steps, share, n_ref, c_ref, packed_ref, wg_ref, wu_ref, wd_ref, pack_ref, sd_ref,
     n_group, c_group, w_group,
-    out_ref, dx_ref, dpack_ref, dsd_ref, n_all, c_all, w_all, og_ref, ou_ref, od_ref, send, recv,
+    out_ref, dx_ref, dpack_ref, dsd_ref, n_all, c_all, w_all, og_out, ou_out, od_out,
+    og_ref, ou_ref, od_ref, send, recv, store,
 ):
     step = pl.program_id(0)
     me = lax.axis_index("expert")
@@ -869,8 +869,16 @@
 
     @pl.when(step == steps - 1)
     def _():
+        copies = [
+            pltpu.make_async_copy(src, dst, store.at[k])
+            for k, (src, dst) in enumerate(((og_ref, og_out), (ou_ref, ou_out), (od_ref, od_out)))
+        ]
+        for copy in copies:
+            copy.start()
         for move in moves:
             move.finish()
+        for copy in copies:
+            copy.wait()
 
 
 def experts(ranks, lanes, normed, cot, packed, turned, w_gate, w_up, w_down, pack, s_down):
@@ -901,8 +909,7 @@
             rows(width),
             pl.BlockSpec(pack.shape, lambda i: (0, 0)),
             pl.BlockSpec((share, width), lambda i: (0, 0)),
-            anywhere, anywhere, anywhere,
-            *(pl.BlockSpec(a.shape[1:], lambda i: (0, 0), pipeline_mode=pl.Buffered(1)) for a in fixed[:3]),
+            *([anywhere] * 6),
         ],
         out_shape=[
             shape((total, width), BF),
@@ -914,7 +921,10 @@
             shape((6, TURNED, total // 2), BF),
             *(shape(a.shape[1:], F32) for a in fixed[:3]),
         ],
-        scratch_shapes=[dma((3, Across.SEMAPHORES)), dma((3, Across.SEMAPHORES))],
+        scratch_shapes=[
+            *(pltpu.VMEM(a.shape[1:], F32) for a in fixed[:3]),
+            dma((3, Across.SEMAPHORES)), dma((3, Across.SEMAPHORES)), dma((3,)),
+        ],
         compiler_params=pltpu.CompilerParams(
             vmem_limit_bytes=VMEM_LIMIT, collective_id=3, has_side_effects=True
         ),

time: 440 us -> 437 us (level)
  transfers between devices with their start and end apart: 4 -> 4, of which waited for: 0 -> 0; matrix products, arithmetic and copies ran while one was open for 1% -> 1% of each run, Pallas kernels for 43% -> 44%
where the time goes in v1:
time: 437 us; the launch traced here: 429 us
  Pallas kernels  396 us (91%)
  between operations  14.4 us (3%)
  local copies, waits for them, and re-layouts  7.91 us (2%)
  other arithmetic  6.96 us (2%)
    pallas_call x1, Pallas kernels, tail(): pl.pallas_call(functools.partial(tail_kernel, ranks, groups, heads, slots...  87.9 us
    pallas_call x2, Pallas kernels, expert_weights(): pl.pallas_call(functools.partial(weights_kernel, j, count, first, size, o...  82.8 us
    pallas_call x1, Pallas kernels, front(): pl.pallas_call(functools.partial(front_kernel, ranks, groups, heads, seqs...  72.1 us
    pallas_call x1, Pallas kernels, experts(): pl.pallas_call(functools.partial(experts_kernel, ranks, count, steps, sha...  66.9 us
    pallas_call x1, Pallas kernels, project(): pl.pallas_call(functools.partial(project_kernel, ranks, groups, heads, sl...  55.1 us
    pallas_call x1, Pallas kernels, vmem_call(): pl.pallas_call(kernel, out_shape=outs, in_specs=[spec] * len(args), out_s...  18.3 us
    pallas_call x1, Pallas kernels, outputs(): pl.pallas_call(functools.partial(outputs_kernel, heads, slots, j, gain_at...  12.4 us
  transfers between devices with their start and end apart: 4, of which 0 were waited for; matrix products, arithmetic and copies ran while one was open for 1% of the time, Pallas kernels for 44%

profile of v1, /device:TPU:13, one launch (start us, length us, event | category | flops | bytes accessed | tf_op | source)
XLA Modules:
  0.0 429.2 jit_solution(14691067495050268763)
XLA Ops:
  7.2 0.0 reduce-scatter.3.cloned.1.call-start
  7.2 0.7 broadcast_in_dim.38
  7.9 0.7 broadcast_in_dim.39
  8.5 0.7 pad_maximum_fusion
  9.2 0.7 copy.48.rest_ref
  10.0 1.4 copy.47
  11.4 72.1 %front.1 = (bf16[8,128,1280]{2,1,0:T(8,128)(2,1)}, bf16[8,128,1408]{2,1,0:T(8,128)(2,1)}, bf16[1280,256]{1,0:T(8,128)(2,1)}, bf16[1280,256]{1,0:T(8,128)(2,1)}, ...) custom-call(bf16[128,1280]{1,0:T(8,128)(2,1)} %bitcast.23, ...), custom_call_target="tpu_custom_call" | custom-call | tf_op jit(solution)/shard_map/front/pallas_call | solution.py:452
  83.6 55.1 %project.1 = (f32[128,1280]{1,0:T(8,128)}, bf16[1024,1280]{1,0:T(8,128)(2,1)}, bf16[1024,1280]{1,0:T(8,128)(2,1)}, bf16[1280,1280]{1,0:T(8,128)(2,1)}, bf16[1024...) custom-call(bf16[8,128,1280]{2,1,0:T(8,128)(2,1)} %get-tuple-element.91.x_ref, ...), custom_call_target="tpu_custom_call" | custom-call | tf_op jit(solution)/shard_map/project/pallas_call | solution.py:606
  138.6 66.9 %experts.1 = (bf16[1024,1280]{1,0:T(8,128)(2,1)}, bf16[1024,1280]{1,0:T(8,128)(2,1)}, f32[1280,256]{1,0:T(8,128)}, f32[112,1280]{1,0:T(8,128)}, bf16[6,512,1280]...) custom-call(bf16[1024,1280]{1,0:T(8,128)(2,1)} %get-tuple-element.11, ...), custom_call_target="tpu_custom_call" | custom-call | flops 28185722880 | bytes 31457280 | tf_op jit(solution)/shard_map/experts/pallas_call | solution.py:903
  205.6 0.0 copy-start
  205.6 0.0 reduce-scatter.3.cloned.1.call-update
  205.6 0.0 all-gather.2.cloned.1.call-start
  205.6 0.9 slice_reduce_fusion.2
  206.5 0.2 copy-done
  206.7 0.1 multiply_reduce_fusion
  206.8 0.0 copy-start.2
  206.8 42.3 %expert_weights.2 = (f32[2,1280,896]{2,1,0:T(8,128)}, f32[2,1280,896]{2,1,0:T(8,128)}, f32[2,896,1280]{2,1,0:T(8,128)}) custom-call(bf16[1024,1280]{1,0:T(8,128)(2,1)} %get-tuple-element.110.n_ref.n_group.n_own, bf16[1024,1408]{1,0:T(8,128)(2,1)} %bitcast.21, bf16[1024,128]{1,0:T(8,128)(2,1)} %get-tuple-element.112.packed_ref.packed_own, ...), custom_call_target="tpu_custom_call" | custom-call | flops 32212254720 | bytes 41943040 | tf_op jit(solution)/shard_map/expert_weights/pallas_call | solution.py:1029
  249.1 0.0 copy-start.3
  249.1 0.0 reduce-scatter.3.cloned.1.call-done
  249.2 1.3 fusion.6
  250.4 0.0 copy-done.2
  250.4 2.2 fusion.9
  252.6 0.0 all-gather.2.cloned.1.call-update
  252.6 0.0 all-reduce.3.cloned.1.call-start
  252.7 0.0 copy-done.3
  252.7 0.7 convert_element_type.23
  253.4 40.5 %expert_weights.3 = (f32[2,1280,896]{2,1,0:T(8,128)}, f32[2,1280,896]{2,1,0:T(8,128)}, f32[2,896,1280]{2,1,0:T(8,128)}) custom-call(bf16[1024,1280]{1,0:T(8,128)(2,1)} %get-tuple-element.110.n_ref.n_group.n_own, bf16[1024,1408]{1,0:T(8,128)(2,1)} %bitcast.22, ...), custom_call_target="tpu_custom_call", output_to_operand_aliasing={{0}: (10, {}), {1}: (11, {}), {2}: (12, {})} | custom-call | flops 24159191040 | bytes 41943040 | tf_op jit(solution)/shard_map/expert_weights/pallas_call | solution.py:1029
  293.9 0.0 all-gather.2.cloned.1.call-done.da_ref
  294.0 3.5 convolution_convert_fusion
  297.5 0.0 all-reduce.3.cloned.1.call-update
  297.5 0.3 reduce-scatter.5.cloned.1.call-start
  297.8 0.3 reduce-scatter.5.cloned.1.call-update
  298.1 0.0 copy-start.1
  298.1 18.3 %attend_back.1 = (bf16[1024,1280]{1,0:T(8,128)(2,1)}, bf16[1280,256]{1,0:T(8,128)(2,1)}, bf16[1280,256]{1,0:T(8,128)(2,1)}, bf16[1280,256]{1,0:T(8,128)(2,1)}, f32[1,1280]{1,0:T(1,128)}) custom-call(bf16[1024,1280]{1,0:T(8,128)(2,1)} %all-gather.2.cloned.1.call-done.da_ref, bf16[1024,1280]{1,0:T(8,128)(2,1)} %bitcast.17, ...), custom_call_target="tpu_custom_call" | custom-call | tf_op jit(solution)/shard_map/attend_back/pallas_call | solution.py:55
  316.4 0.7 reduce.1
  317.1 0.0 copy-done.1
  317.1 1.2 select_convert_fusion.dpack_ref
  318.3 87.9 %tail.1 = (f32[128,1280]{1,0:T(8,128)}, bf16[4,8,160,256]{3,2,1,0:T(8,128)(2,1)}, bf16[1280,896]{1,0:T(8,128)(2,1)}, bf16[1280,896]{1,0:T(8,128)(2,1)}, bf16[896,1280]{1,0:T(8,128)(2,1)}) custom-call(bf16[4,2,128,1280]{3,2,1,0:T(8,128)(2,1)} %bitcast.29, bf16[1280,256]{1,0:T(8,128)(2,1)} %get-tuple-element.134.dwq_ref, ...), custom_call_target="tpu_custom_call" | custom-call | flops 56371445760 | bytes 67108864 | tf_op jit(solution)/shard_map/tail/pallas_call | solution.py:1332
  406.2 0.0 all-reduce.3.cloned.1.call-done
  406.3 0.0 reduce-scatter.5.cloned.1.call-done.out_ref
  406.3 12.4 %outputs.1 = (bf16[128,1280]{1,0:T(8,128)(2,1)}, bf16[128,1280]{1,0:T(8,128)(2,1)}, f32[160,1280]{1,0:T(8,128)}, f32[160,1280]{1,0:T(8,128)}, f32[160,1280]{1,0:...) custom-call(f32[128,1280]{1,0:T(8,128)} %get-tuple-element.142.dn_re, ...), custom_call_target="tpu_custom_call", output_to_operand_aliasing={{10}: (12, {}), {11}: (13, {}), {12}: (14, {})} | custom-call | tf_op jit(solution)/shard_map/outputs/pallas_call | solution.py:1413
  418.7 1.8 slice_reduce_fusion
  420.5 1.0 slice.15
  421.4 0.7 copy.49
  (3 shorter events, 0.0 us)
Async XLA Ops:
  7.2 242.0 %reduce-scatter.3.cloned.1.call-start = ((), (), s32[]{:S(2)}) async-start(), calls=%async_computation.2 | async-start | bytes 2949120 | tf_op jit(solution)/shard_map/reduce_scatter | solution.py:1495
  205.6 1.1 copy-start
  205.6 88.4 %all-gather.2.cloned.1.call-start = ((), (), s32[]{:S(2)}) async-start(), calls=%async_computation.3 | async-start | bytes 2949120 | tf_op jit(solution)/shard_map/all_gather | solution.py:1505
  206.8 43.6 %copy-start.2 = (bf16[1,128,1280]{2,1,0:T(8,128)(2,1)S(1)}, bf16[1,128,1280]{2,1,0:T(8,128)(2,1)}, u32[]{:S(2)}) copy-start(bf16[1,128,1280]{2,1,0:T(8,128)(2,1)} %param.19) | copy-start | bytes 983044
  249.1 3.5 copy-start.3
  252.6 153.6 %all-reduce.3.cloned.1.call-start = ((), (), s32[]{:S(2)}) async-start(), calls=%async_computation.5 | async-start | bytes 1392640 | tf_op jit(solution)/shard_map/psum | solution.py:1518
  297.5 108.8 %reduce-scatter.5.cloned.1.call-start = ((), (), s32[]{:S(2)}) async-start(), calls=%async_computation.4 | async-start | bytes 2949120 | tf_op jit(solution)/shard_map/reduce_scatter | solution.py:1495
  298.1 19.0 %copy-start.1 = (f32[1280,256]{1,0:T(8,128)S(1)}, f32[1280,256]{1,0:T(8,128)}, u32[]{:S(2)}) copy-start(f32[1280,256]{1,0:T(8,128)} %get-tuple-element.138) | copy-start | bytes 3932164
Sparse Core Ops, SparseCore 0:
  205.7 33.2 reduce-scatter.2
  252.7 33.7 all-gather.1
  297.6 52.7 all-reduce.2
  352.7 42.9 reduce-scatter.4
